TPU v7x, 512 devices: a whole 4x8x8 slice. The times are simulated.
512 devices in a mesh: section: 32 (over x, y), tensor: 16 (over z, core).
Axes of the slice: x: 4, y: 8, z: 8, core: 2. Of those that a mesh axis runs over, the one named last changes fastest.
Arguments:
- frozen: bfloat16 [32, 14336, 2048], P('section', 'tensor'), may hold values from -1 to 1, as said below
- adapter_a: bfloat16 [32, 8, 14336], P('section', None, 'tensor'), may hold values from -0.119628906 to 0.119628906
- adapter_b: bfloat16 [32, 16, 2048], P('section'), may hold values from -0.22460938 to 0.22460938
- magnitude: float32 [32, 2048], P('section'), may hold values from 0.5 to 2
- hidden_fwd: bfloat16 [32, 128, 14336], P('section', None, 'tensor'), may hold values from -6 to 6
- carried: bfloat16 [32, 256, 2048], P('section', 'tensor'), may hold values from -6 to 6
- embedded: bfloat16 [256, 4096], P('tensor'), may hold values from -6 to 6
- hidden_bwd: bfloat16 [32, 128, 14336], P('section', None, 'tensor'), may hold values from -6 to 6
- returned: bfloat16 [32, 256, 2048], P('section', 'tensor'), may hold values from -1.5 to 1.5
- head_grad: bfloat16 [256, 4096], P('tensor'), may hold values from -1.5 to 1.5
Outputs:
- section_out: bfloat16 [32, 256, 2048], P('section', 'tensor')
- grad_magnitude: float32 [32, 2048], P('section')
- grad_a: float32 [32, 8, 14336], P('section', None, 'tensor')
- grad_b: float32 [32, 16, 2048], P('section')
- hidden_grad: bfloat16 [32, 128, 14336], P('section', None, 'tensor')
Inputs may be any that keep to these rules, and one draw needn't show every extreme that they name: frozen projection weights.
All inputs are finite; a program needn't handle non-finite values.
Results may differ from a plain program's by a relative error of at most 0.0057.
Values may be sent and summed in bfloat16 or wider, within the bound.
A program may use at most 64 MiB of HBM per device.

v0:
```python
import jax
import jax.numpy as jnp
from jax import lax
from jax.sharding import PartitionSpec as P

epsilon = 1e-06


def swapped(array, axis, apart):
    return lax.ppermute(array, axis, [(i, i ^ 1 << apart) for i in range(lax.axis_size(axis))])


def from_behind(array, axis, by):
    count = lax.axis_size(axis)
    pairs = [(i, i + by) for i in range(count) if 0 <= i + by < count]
    return lax.ppermute(array, axis, pairs)


def column_norms(squares):
    return jnp.sqrt(lax.psum(squares, "tensor") + epsilon)


def forward_rows(term_fn, own_rows):
    return lax.psum_scatter(
        term_fn(jnp.int32(0), own_rows * lax.axis_size("tensor")),
        "tensor",
        scatter_dimension=0,
        tiled=True,
    )


def local(
    frozen,
    adapter_a,
    adapter_b,
    magnitude,
    hidden_fwd,
    carried,
    embedded,
    hidden_bwd,
    returned,
    head_grad,
):
    base_w = frozen[0]
    fac_half = adapter_a[0]
    fac_b = adapter_b[0]
    mag = magnitude[0]
    own_rows = carried.shape[1]
    slot_id = lax.axis_index("section")
    slot_count = lax.axis_size("section")
    half = slot_id % 2
    first_half = half == 0
    fwd_other, bwd_other, fac_other = swapped(
        (hidden_fwd[0], hidden_bwd[0], fac_half), "section", 0
    )

    def in_order(own, other):
        return jnp.concatenate(
            [jnp.where(first_half, own, other), jnp.where(first_half, other, own)], axis=0
        )

    hid_fwd = in_order(hidden_fwd[0], fwd_other)
    hid_bwd = in_order(hidden_bwd[0], bwd_other)
    fac_a = in_order(fac_half, fac_other)
    width = base_w.shape[1]
    arriving = from_behind(carried[0], "section", 2)
    embed_cols = lax.dynamic_slice_in_dim(embedded, half * width, width, 1)
    inflow = jnp.where(slot_id < 2, embed_cols, arriving)
    coming = from_behind(returned[0], "section", -2)
    head_cols = lax.dynamic_slice_in_dim(head_grad, half * width, width, 1)
    cotangent = jnp.where(slot_id >= slot_count - 2, head_cols, coming)
    merged = (
        base_w.astype(jnp.float32)
        + jnp.einsum("rf,rd->fd", fac_a, fac_b, preferred_element_type=jnp.float32)
    ).astype(jnp.bfloat16)
    merged_f = merged.astype(jnp.float32)
    squares = jnp.sum(merged_f * merged_f, axis=0)
    low_part = jnp.einsum("tf,rf->tr", hid_bwd, fac_a, preferred_element_type=jnp.float32)
    low = lax.psum(low_part, "tensor").astype(jnp.bfloat16)
    col_norms = column_norms(squares)
    col_scale = mag / col_norms

    def scaled_term(offset, amount):
        return jnp.dot(hid_fwd, merged, preferred_element_type=jnp.float32) * col_scale

    projected = forward_rows(scaled_term, own_rows)
    section_out = (inflow.astype(jnp.float32) + projected).astype(jnp.bfloat16)
    all_rows = hid_bwd.shape[0]
    mag_acc = jnp.zeros((width,), jnp.float32)
    scaled_cot = (
        lax.all_gather(cotangent, "tensor", axis=0, tiled=True).astype(jnp.float32) * col_scale
    ).astype(jnp.bfloat16)
    hid_part = jnp.einsum("td,fd->tf", scaled_cot, merged, preferred_element_type=jnp.float32)
    hid_acc = hid_part
    adapt_part = jnp.einsum("td,rd->tr", scaled_cot, fac_b, preferred_element_type=jnp.float32)
    adapt_acc = adapt_part
    grad_b_acc = jnp.einsum("tr,td->rd", low, scaled_cot, preferred_element_type=jnp.float32)
    hid_acc, adapt_acc, grad_b_acc, mag_acc = (hid_acc, adapt_acc, grad_b_acc, mag_acc)
    half_rows = all_rows // 2
    send_hid = lax.dynamic_slice_in_dim(hid_acc, (1 - half) * half_rows, half_rows, 0)
    got_hid, got_adapt = swapped((send_hid, adapt_acc), "section", 0)
    own_hid = lax.dynamic_slice_in_dim(hid_acc, half * half_rows, half_rows, 0)
    hidden_grad = (own_hid + got_hid).astype(jnp.bfloat16)
    adapter_cot = (adapt_acc + got_adapt).astype(jnp.bfloat16)
    rank_half = fac_half.shape[0]
    own_cot = lax.dynamic_slice_in_dim(adapter_cot, half * rank_half, rank_half, 1)
    grad_a = jnp.einsum("tr,tf->rf", own_cot, hid_bwd, preferred_element_type=jnp.float32)
    own_recomputed = lax.psum_scatter(
        jnp.dot(hid_bwd, merged, preferred_element_type=jnp.float32),
        "tensor",
        scatter_dimension=0,
        tiled=True,
    )
    mag_part = jnp.sum(cotangent.astype(jnp.float32) * own_recomputed, axis=0)
    grad_mag = lax.psum(mag_part, "tensor") / col_norms
    return (section_out[None], grad_mag[None], grad_a[None], grad_b_acc[None], hidden_grad[None])


def solution(mesh):
    placed = (
        P("section", "tensor", None),
        P("section", None, "tensor"),
        P("section", None, None),
        P("section", None),
        P("section", None, "tensor"),
        P("section", "tensor", None),
        P("tensor", None),
        P("section", None, "tensor"),
        P("section", "tensor", None),
        P("tensor", None),
    )
    return jax.shard_map(
        local,
        mesh=mesh,
        in_specs=placed,
        out_specs=(
            P("section", "tensor", None),
            P("section", None),
            P("section", None, "tensor"),
            P("section", None, None),
            P("section", None, "tensor"),
        ),
        check_vma=False,
    )
```

profile of v0, /device:TPU:2, one launch (start us, length us, event | category | flops | bytes accessed | tf_op | source)
XLA Modules:
  0.0 222.4 jit_solution(7242099458020499546)
XLA Ops:
  7.2 3.5 %collective-permute-start.2 = (bf16[8,896]{1,0:T(8,128)(2,1)}, bf16[8,896]{1,0:T(8,128)(2,1)S(1)}, u32[]{:S(2)}, u32[]{:S(2)}) collective-permute-start(bf16[8,896]{1,0:T(8,128)(2,1)} %bitcast.37), channel_id=1, source_target_pairs={{0,16},{16,0},{32,48},{48,32},{64,80},{80,64},{96,112},{112,96},{1... | collective-permute-start | bytes 43016 | tf_op jit(solution)/shard_map/ppermute | solution.py:10
  10.7 2.4 %collective-permute-start.4 = (bf16[128,896]{1,0:T(8,128)(2,1)}, bf16[128,896]{1,0:T(8,128)(2,1)S(1)}, u32[]{:S(2)}, u32[]{:S(2)}) collective-permute-start(bf16[128,896]{1,0:T(8,128)(2,1)} %bitcast.35), channel_id=1, source_target_pairs={{0,16},{16,0},{32,48},{48,32},{64,80},{80,64},{96,112},{112,96},{1... | collective-permute-start | bytes 688136 | tf_op jit(solution)/shard_map/ppermute | solution.py:10
  13.8 3.4 %multiply_reduce_fusion = (f32[2048]{0:T(1024)S(1)}, bf16[896,2048]{1,0:T(8,128)(2,1)S(1)}) fusion(bf16[1,16,2048]{2,1,0:T(8,128)(2,1)S(1)} %copy-done, bf16[8,896]{1,0:T(8,128)(2,1)S(1)} %get-tuple-element.15, bf16[8,896]{1,0:T(8,128)(2,1)S(1)} %get-tuple-element.14, bf16[1,896,2048]{2,1,0:T(8,128)(2,1)} %param.10), kind=kOutput, calls=%fused_computation.2 | convolution fusion | flops 69785600 | bytes 7442432 | tf_op jit(solution)/shard_map/rf,rd->fd/dot_general | solution.py:74
  17.2 2.7 %collective-permute-done.4 = bf16[128,896]{1,0:T(8,128)(2,1)S(1)} collective-permute-done((bf16[128,896]{1,0:T(8,128)(2,1)}, bf16[128,896]{1,0:T(8,128)(2,1)S(1)}, u32[]{:S(2)}, u32[]{:S(2)}) %collective-permute-start.4) | collective-permute-done | bytes 229408 | tf_op jit(solution)/shard_map/ppermute | solution.py:10
  20.0 2.6 %fusion.8 = f32[256,2048]{1,0:T(8,128)} fusion(bf16[896,2048]{1,0:T(8,128)(2,1)S(1)} %get-tuple-element.19, bf16[128,896]{1,0:T(8,128)(2,1)S(1)} %get-tuple-element.13, bf16[128,896]{1,0:T(8,128)(2,1)S(1)} %get-tuple-element.12), kind=kOutput, calls=%fused_computation.20 | convolution fusion | flops 940441600 | bytes 6225920 | tf_op jit(solution)/shard_map/dot_general | solution.py:109
  22.7 5.2 %collective-permute-start.3 = (bf16[16,2048]{1,0:T(8,128)(2,1)S(1)}, bf16[16,2048]{1,0:T(8,128)(2,1)S(1)}, u32[]{:S(2)}, u32[]{:S(2)}) collective-permute-start(bf16[16,2048]{1,0:T(8,128)(2,1)S(1)} %bitcast.40), channel_id=1, source_target_pairs={{32,0},{48,16},{64,32},{80,48},{96,64},{112,80},{128,96},{144,112}... | collective-permute-start | bytes 196616 | tf_op jit(solution)/shard_map/ppermute | solution.py:16
  28.0 2.5 %collective-permute-done.3 = bf16[16,2048]{1,0:T(8,128)(2,1)S(1)} collective-permute-done((bf16[16,2048]{1,0:T(8,128)(2,1)S(1)}, bf16[16,2048]{1,0:T(8,128)(2,1)S(1)}, u32[]{:S(2)}, u32[]{:S(2)}) %collective-permute-start.3) | collective-permute-done | bytes 65568 | tf_op jit(solution)/shard_map/ppermute | solution.py:16
  30.5 58.6 %reduce-scatter.5.cloned.1.call-done = f32[16,2048]{1,0:T(8,128)} async-done(((f32[256,2048]{1,0:T(8,128)}), f32[16,2048]{1,0:T(8,128)}) %reduce-scatter.5.cloned.1.call-update) | async-done | bytes 131088 | tf_op jit(solution)/shard_map/reduce_scatter | solution.py:108
  89.1 1.6 multiply_reduce_fusion.1
  90.8 3.6 %collective-permute-start.1 = (bf16[128,896]{1,0:T(8,128)(2,1)S(1)}, bf16[128,896]{1,0:T(8,128)(2,1)S(1)}, u32[]{:S(2)}, u32[]{:S(2)}) collective-permute-start(bf16[128,896]{1,0:T(8,128)(2,1)S(1)} %bitcast.36), channel_id=1, source_target_pairs={{0,16},{16,0},{32,48},{48,32},{64,80},{80,64},{96,112},{112,96},{1... | collective-permute-start | bytes 688136 | tf_op jit(solution)/shard_map/ppermute | solution.py:10
  94.6 4.1 %collective-permute-done.1 = bf16[128,896]{1,0:T(8,128)(2,1)S(1)} collective-permute-done((bf16[128,896]{1,0:T(8,128)(2,1)S(1)}, bf16[128,896]{1,0:T(8,128)(2,1)S(1)}, u32[]{:S(2)}, u32[]{:S(2)}) %collective-permute-start.1) | collective-permute-done | bytes 229408 | tf_op jit(solution)/shard_map/ppermute | solution.py:10
  98.7 50.0 %all-reduce = (f32[2048]{0:T(1024)S(1)}, f32[2048]{0:T(1024)S(1)}, bf16[256,16]{1,0:T(8,128)(2,1)S(1)}) all-reduce(f32[2048]{0:T(1024)S(1)} %get-tuple-element.18, f32[2048]{0:T(1024)S(1)} %get-tuple-element.8, f32[256,16]{1,0:T(8,128)S(1)} %fusion.7), channel_id=1, replica_groups=mesh['section'=32,'tensor'=16] {'tensor'}, use_global_device_ids=true, to_apply=%region_1.2 | all-reduce | flops 8192 | bytes 57344 | tf_op jit(solution)/shard_map/psum | solution.py:20
  149.4 4.6 %convolution_multiply_fusion = f32[256,2048]{1,0:T(8,128)} fusion(bf16[896,2048]{1,0:T(8,128)(2,1)} %copy-done.1, f32[2048]{0:T(1024)S(1)} %get-tuple-element.17, bf16[128,896]{1,0:T(8,128)(2,1)S(1)} %get-tuple-element.11, bf16[128,896]{1,0:T(8,128)(2,1)S(1)} %get-tuple-element.10), kind=kOutput, calls=%fused_computation.3 | convolution fusion | flops 940965888 | bytes 6234112 | tf_op jit(solution)/shard_map/dot_general | solution.py:84
  154.1 3.7 %fusion.1 = f32[256,896]{1,0:T(8,128)S(1)} fusion(bf16[896,2048]{1,0:T(8,128)(2,1)} %copy-done.1, bf16[256,2048]{1,0:T(8,128)(2,1)} %all-gather.2.cloned.1.call-done, f32[2048]{0:T(1024)S(1)} %get-tuple-element.17), kind=kOutput, calls=%fused_computation.7 | convolution fusion | flops 941096960 | bytes 5644288 | tf_op jit(solution)/shard_map/td,fd->tf/dot_general | solution.py:93
  157.9 3.4 %collective-permute-start.6 = (f32[128,896]{1,0:T(8,128)S(1)}, f32[128,896]{1,0:T(8,128)S(1)}, u32[]{:S(2)}, u32[]{:S(2)}) collective-permute-start(f32[128,896]{1,0:T(8,128)S(1)} %constant_dynamic-slice_fusion), channel_id=1, source_target_pairs={{0,16},{16,0},{32,48},{48,32},{64,80},{80,64},{96,112},{112,96},{1... | collective-permute-start | bytes 1376264 | tf_op jit(solution)/shard_map/ppermute | solution.py:10
  161.2 4.3 %collective-permute-start = (bf16[16,2048]{1,0:T(8,128)(2,1)}, bf16[16,2048]{1,0:T(8,128)(2,1)S(1)}, u32[]{:S(2)}, u32[]{:S(2)}) collective-permute-start(bf16[16,2048]{1,0:T(8,128)(2,1)} %bitcast), channel_id=1, source_target_pairs={{0,32},{16,48},{32,64},{48,80},{64,96},{80,112},{96,128},{112,144}... | collective-permute-start | bytes 196616 | tf_op jit(solution)/shard_map/ppermute | solution.py:16
  166.0 2.5 %collective-permute-start.5 = (f32[256,16]{0,1:T(8,128)S(1)}, f32[256,16]{0,1:T(8,128)S(1)}, u32[]{:S(2)}, u32[]{:S(2)}) collective-permute-start(f32[256,16]{0,1:T(8,128)S(1)} %fusion.2), channel_id=1, source_target_pairs={{0,16},{16,0},{32,48},{48,32},{64,80},{80,64},{96,112},{112,96},{1... | collective-permute-start | bytes 49160 | tf_op jit(solution)/shard_map/ppermute | solution.py:10
  168.4 1.0 convolution_bitcast_fusion
  169.4 2.2 collective-permute-done.5
  171.6 0.8 convolution_bitcast_fusion.1
  172.4 0.7 fusion.6
  173.1 1.3 collective-permute-done
  174.5 39.8 %reduce-scatter.3.cloned.1.call-done = f32[16,2048]{1,0:T(8,128)} async-done(((f32[256,2048]{1,0:T(8,128)}), f32[16,2048]{1,0:T(8,128)}) %reduce-scatter.3.cloned.1.call-update) | async-done | bytes 131088 | tf_op jit(solution)/shard_map/reduce_scatter | solution.py:24
  214.3 1.6 fusion.9
  (32 shorter events, 2.4 us)
Async XLA Ops:
  7.2 6.7 %copy-start = (bf16[1,16,2048]{2,1,0:T(8,128)(2,1)S(1)}, bf16[1,16,2048]{2,1,0:T(8,128)(2,1)}, u32[]{:S(2)}) copy-start(bf16[1,16,2048]{2,1,0:T(8,128)(2,1)} %param.12) | copy-start | bytes 196612
  7.2 81.9 %reduce-scatter.5.cloned.1.call-start = ((), (), s32[]{:S(2)}) async-start(), calls=%async_computation.3 | async-start | bytes 2228224 | tf_op jit(solution)/shard_map/reduce_scatter | solution.py:108
  7.2 5.9 %collective-permute-start.2 = (bf16[8,896]{1,0:T(8,128)(2,1)}, bf16[8,896]{1,0:T(8,128)(2,1)S(1)}, u32[]{:S(2)}, u32[]{:S(2)}) collective-permute-start(bf16[8,896]{1,0:T(8,128)(2,1)} %bitcast.37), channel_id=1, source_target_pairs={{0,16},{16,0},{32,48},{48,32},{64,80},{80,64},{96,112},{112,96},{1... | collective-permute-start | bytes 43016 | tf_op jit(solution)/shard_map/ppermute | solution.py:10
  10.7 9.2 %collective-permute-start.4 = (bf16[128,896]{1,0:T(8,128)(2,1)}, bf16[128,896]{1,0:T(8,128)(2,1)S(1)}, u32[]{:S(2)}, u32[]{:S(2)}) collective-permute-start(bf16[128,896]{1,0:T(8,128)(2,1)} %bitcast.35), channel_id=1, source_target_pairs={{0,16},{16,0},{32,48},{48,32},{64,80},{80,64},{96,112},{112,96},{1... | collective-permute-start | bytes 688136 | tf_op jit(solution)/shard_map/ppermute | solution.py:10
  13.8 6.1 %copy-start.3 = (bf16[1,128,896]{2,1,0:T(8,128)(2,1)S(1)}, bf16[1,128,896]{2,1,0:T(8,128)(2,1)}, u32[]{:S(2)}) copy-start(bf16[1,128,896]{2,1,0:T(8,128)(2,1)} %param.17) | copy-start | bytes 688132
  17.2 2.7 %copy-start.1 = (bf16[896,2048]{1,0:T(8,128)(2,1)}, bf16[896,2048]{1,0:T(8,128)(2,1)S(1)}, u32[]{:S(2)}) copy-start(bf16[896,2048]{1,0:T(8,128)(2,1)S(1)} %get-tuple-element.19) | copy-start | bytes 11010052
  20.0 2.8 %copy-start.7 = (bf16[1,16,2048]{2,1,0:T(8,128)(2,1)S(1)}, bf16[1,16,2048]{2,1,0:T(8,128)(2,1)}, u32[]{:S(2)}) copy-start(bf16[1,16,2048]{2,1,0:T(8,128)(2,1)} %param.18) | copy-start | bytes 196612
  20.0 69.1 %copy-start.5 = (bf16[16,4096]{1,0:T(8,128)(2,1)S(1)}, bf16[16,4096]{1,0:T(8,128)(2,1)}, u32[]{:S(2)}) copy-start(bf16[16,4096]{1,0:T(8,128)(2,1)} %param.19) | copy-start | bytes 393220
  20.0 70.8 %copy-start.4 = (bf16[1,128,896]{2,1,0:T(8,128)(2,1)S(1)}, bf16[1,128,896]{2,1,0:T(8,128)(2,1)}, u32[]{:S(2)}) copy-start(bf16[1,128,896]{2,1,0:T(8,128)(2,1)} %param.14) | copy-start | bytes 688132
  22.6 126.1 %copy-start.6 = (f32[1,2048]{1,0:T(1,128)S(1)}, f32[1,2048]{1,0:T(1,128)}, u32[]{:S(2)}) copy-start(f32[1,2048]{1,0:T(1,128)} %param.13) | copy-start | bytes 24580
  22.7 131.4 %all-gather.2.cloned.1.call-start = ((), (), s32[]{:S(2)}) async-start(), calls=%async_computation.4 | async-start | bytes 1114112 | tf_op jit(solution)/shard_map/all_gather | solution.py:91
  22.7 7.8 %collective-permute-start.3 = (bf16[16,2048]{1,0:T(8,128)(2,1)S(1)}, bf16[16,2048]{1,0:T(8,128)(2,1)S(1)}, u32[]{:S(2)}, u32[]{:S(2)}) collective-permute-start(bf16[16,2048]{1,0:T(8,128)(2,1)S(1)} %bitcast.40), channel_id=1, source_target_pairs={{32,0},{48,16},{64,32},{80,48},{96,64},{112,80},{128,96},{144,112}... | collective-permute-start | bytes 196616 | tf_op jit(solution)/shard_map/ppermute | solution.py:16
  90.7 123.6 %reduce-scatter.3.cloned.1.call-start = ((), (), s32[]{:S(2)}) async-start(), calls=%async_computation.2 | async-start | bytes 2228224 | tf_op jit(solution)/shard_map/reduce_scatter | solution.py:24
  90.8 7.9 %collective-permute-start.1 = (bf16[128,896]{1,0:T(8,128)(2,1)S(1)}, bf16[128,896]{1,0:T(8,128)(2,1)S(1)}, u32[]{:S(2)}, u32[]{:S(2)}) collective-permute-start(bf16[128,896]{1,0:T(8,128)(2,1)S(1)} %bitcast.36), channel_id=1, source_target_pairs={{0,16},{16,0},{32,48},{48,32},{64,80},{80,64},{96,112},{112,96},{1... | collective-permute-start | bytes 688136 | tf_op jit(solution)/shard_map/ppermute | solution.py:10
  154.1 11.5 %copy-start.2 = (bf16[256,2048]{1,0:T(8,128)(2,1)S(1)}, bf16[256,2048]{1,0:T(8,128)(2,1)}, u32[]{:S(2)}) copy-start(bf16[256,2048]{1,0:T(8,128)(2,1)} %all-gather.2.cloned.1.call-done) | copy-start | bytes 3145732
  157.9 14.5 %collective-permute-start.6 = (f32[128,896]{1,0:T(8,128)S(1)}, f32[128,896]{1,0:T(8,128)S(1)}, u32[]{:S(2)}, u32[]{:S(2)}) collective-permute-start(f32[128,896]{1,0:T(8,128)S(1)} %constant_dynamic-slice_fusion), channel_id=1, source_target_pairs={{0,16},{16,0},{32,48},{48,32},{64,80},{80,64},{96,112},{112,96},{1... | collective-permute-start | bytes 1376264 | tf_op jit(solution)/shard_map/ppermute | solution.py:10
  161.2 13.2 %collective-permute-start = (bf16[16,2048]{1,0:T(8,128)(2,1)}, bf16[16,2048]{1,0:T(8,128)(2,1)S(1)}, u32[]{:S(2)}, u32[]{:S(2)}) collective-permute-start(bf16[16,2048]{1,0:T(8,128)(2,1)} %bitcast), channel_id=1, source_target_pairs={{0,32},{16,48},{32,64},{48,80},{64,96},{80,112},{96,128},{112,144}... | collective-permute-start | bytes 196616 | tf_op jit(solution)/shard_map/ppermute | solution.py:16
  166.0 5.6 %collective-permute-start.5 = (f32[256,16]{0,1:T(8,128)S(1)}, f32[256,16]{0,1:T(8,128)S(1)}, u32[]{:S(2)}, u32[]{:S(2)}) collective-permute-start(f32[256,16]{0,1:T(8,128)S(1)} %fusion.2), channel_id=1, source_target_pairs={{0,16},{16,0},{32,48},{48,32},{64,80},{80,64},{96,112},{112,96},{1... | collective-permute-start | bytes 49160 | tf_op jit(solution)/shard_map/ppermute | solution.py:10
Sparse Core Ops, SparseCore 0:
  22.8 66.2 reduce-scatter.4
  91.8 40.0 all-gather.1
  154.2 60.0 reduce-scatter.2
where the time goes:
time: 223 us; the launch traced here: 222 us
  waiting for transfers between devices  111 us (50%)
  blocking collectives  50 us (22%)
  starting transfers between devices  24.9 us (11%)
  matrix products  16.7 us (7%)
  between operations  14 us (6%)
  other arithmetic  5.3 us (2%)
    reduce_scatter x1, waiting for transfers between devices, local(): lax.psum_scatter(jnp.dot(hid_bwd, merged, preferred_element_type=jnp.floa...  58.6 us
    psum x1, blocking collectives, column_norms(): return jnp.sqrt(lax.psum(squares, 'tensor') + epsilon)  50 us
    reduce_scatter x1, waiting for transfers between devices, forward_rows(): lax.psum_scatter(term_fn(jnp.int32(0), own_rows * lax.axis_size('tensor')...  39.8 us
    ppermute x5, starting transfers between devices, swapped(): lax.ppermute(array, axis, [(i, i ^ 1 << apart) for i in range(lax.axis_si...  15.2 us
    ppermute x2, starting transfers between devices, from_behind(): return lax.ppermute(array, axis, pairs)  9.55 us
    ppermute x5, waiting for transfers between devices, swapped(): lax.ppermute(array, axis, [(i, i ^ 1 << apart) for i in range(lax.axis_si...  8.95 us
    dot_general x1, matrix products, scaled_term(): jnp.dot(hid_fwd, merged, preferred_element_type=jnp.float32) * col_scale  4.63 us
  transfers between devices with their start and end apart: 10, of which 7 were waited for; matrix products, arithmetic and copies ran while one was open for 7% of the time, Pallas kernels for 0%

commit v1 on v0

--- a/solution.py
+++ b/solution.py
@@ -17,7 +17,7 @@
 
 
 def column_norms(squares):
-    return jnp.sqrt(lax.psum(squares, "tensor") + epsilon)
+    return jnp.sqrt(jnp.sum(lax.all_gather(squares, "tensor"), axis=0) + epsilon)
 
 
 def forward_rows(term_fn, own_rows):

time: 223 us -> 233 us (1.045)
  the two profiles are of different devices: /device:TPU:2 before, /device:TPU:6 now
where the time goes in v1:
time: 233 us
  waiting for transfers between devices  110 us (47%)
  blocking collectives  62.8 us (27%)
  starting transfers between devices  24.4 us (10%)
  matrix products  16.7 us (7%)
  between operations  14 us (6%)
  other arithmetic  5.31 us (2%)
    reduce_scatter x1, waiting for transfers between devices, local(): lax.psum_scatter(jnp.dot(hid_bwd, merged, preferred_element_type=jnp.floa...  58.9 us
    psum x1, blocking collectives, local(): grad_mag = lax.psum(mag_part, 'tensor') / col_norms  48.2 us
    reduce_scatter x1, waiting for transfers between devices, forward_rows(): lax.psum_scatter(term_fn(jnp.int32(0), own_rows * lax.axis_size('tensor')...  40.1 us
    ppermute x5, starting transfers between devices, swapped(): lax.ppermute(array, axis, [(i, i ^ 1 << apart) for i in range(lax.axis_si...  15.2 us
    all_gather x1, blocking collectives, column_norms(): lax.all_gather(squares, 'tensor')  14.5 us
    ppermute x2, starting transfers between devices, from_behind(): return lax.ppermute(array, axis, pairs)  9.15 us
    ppermute x5, waiting for transfers between devices, swapped(): lax.ppermute(array, axis, [(i, i ^ 1 << apart) for i in range(lax.axis_si...  6.3 us
  transfers between devices with their start and end apart: 10, of which 7 were waited for; matrix products, arithmetic and copies ran while one was open for 7% of the time, Pallas kernels for 0%

profile of v1, /device:TPU:6, one launch (start us, length us, event | category | flops | bytes accessed | tf_op | source)
XLA Modules:
  0.0 233.0 jit_solution(5687648987393418745)
XLA Ops:
  7.2 3.5 %collective-permute-start.2 = (bf16[8,896]{1,0:T(8,128)(2,1)}, bf16[8,896]{1,0:T(8,128)(2,1)S(1)}, u32[]{:S(2)}, u32[]{:S(2)}) collective-permute-start(bf16[8,896]{1,0:T(8,128)(2,1)} %bitcast.43), channel_id=1, source_target_pairs={{0,16},{16,0},{32,48},{48,32},{64,80},{80,64},{96,112},{112,96},{1... | collective-permute-start | bytes 43016 | tf_op jit(solution)/shard_map/ppermute | solution.py:10
  10.7 2.4 %collective-permute-start.4 = (bf16[128,896]{1,0:T(8,128)(2,1)}, bf16[128,896]{1,0:T(8,128)(2,1)S(1)}, u32[]{:S(2)}, u32[]{:S(2)}) collective-permute-start(bf16[128,896]{1,0:T(8,128)(2,1)} %bitcast.36), channel_id=1, source_target_pairs={{0,16},{16,0},{32,48},{48,32},{64,80},{80,64},{96,112},{112,96},{1... | collective-permute-start | bytes 688136 | tf_op jit(solution)/shard_map/ppermute | solution.py:10
  13.1 3.5 %collective-permute-start.1 = (bf16[128,896]{1,0:T(8,128)(2,1)}, bf16[128,896]{1,0:T(8,128)(2,1)S(1)}, u32[]{:S(2)}, u32[]{:S(2)}) collective-permute-start(bf16[128,896]{1,0:T(8,128)(2,1)} %bitcast.37), channel_id=1, source_target_pairs={{0,16},{16,0},{32,48},{48,32},{64,80},{80,64},{96,112},{112,96},{1... | collective-permute-start | bytes 688136 | tf_op jit(solution)/shard_map/ppermute | solution.py:10
  17.3 3.4 %multiply_reduce_fusion = (f32[2048]{0:T(1024)S(1)}, bf16[896,2048]{1,0:T(8,128)(2,1)S(1)}) fusion(bf16[1,16,2048]{2,1,0:T(8,128)(2,1)S(1)} %copy-done, bf16[8,896]{1,0:T(8,128)(2,1)S(1)} %get-tuple-element.14, bf16[8,896]{1,0:T(8,128)(2,1)S(1)} %get-tuple-element.13, bf16[1,896,2048]{2,1,0:T(8,128)(2,1)} %param.10), kind=kOutput, calls=%fused_computation.2 | convolution fusion | flops 69785600 | bytes 7442432 | tf_op jit(solution)/shard_map/rf,rd->fd/dot_general | solution.py:74
  21.4 3.5 %collective-permute-done.1 = bf16[128,896]{1,0:T(8,128)(2,1)S(1)} collective-permute-done((bf16[128,896]{1,0:T(8,128)(2,1)}, bf16[128,896]{1,0:T(8,128)(2,1)S(1)}, u32[]{:S(2)}, u32[]{:S(2)}) %collective-permute-start.1) | collective-permute-done | bytes 229408 | tf_op jit(solution)/shard_map/ppermute | solution.py:10
  25.0 2.6 %fusion.8 = f32[256,2048]{1,0:T(8,128)} fusion(bf16[896,2048]{1,0:T(8,128)(2,1)S(1)} %get-tuple-element.18, bf16[128,896]{1,0:T(8,128)(2,1)S(1)} %get-tuple-element.10, bf16[128,896]{1,0:T(8,128)(2,1)S(1)} %get-tuple-element.9), kind=kOutput, calls=%fused_computation.20 | convolution fusion | flops 940441600 | bytes 6225920 | tf_op jit(solution)/shard_map/dot_general | solution.py:109
  27.7 5.5 %collective-permute-start.3 = (bf16[16,2048]{1,0:T(8,128)(2,1)S(1)}, bf16[16,2048]{1,0:T(8,128)(2,1)S(1)}, u32[]{:S(2)}, u32[]{:S(2)}) collective-permute-start(bf16[16,2048]{1,0:T(8,128)(2,1)S(1)} %bitcast.45), channel_id=1, source_target_pairs={{32,0},{48,16},{64,32},{80,48},{96,64},{112,80},{128,96},{144,112}... | collective-permute-start | bytes 196616 | tf_op jit(solution)/shard_map/ppermute | solution.py:16
  33.2 2.1 collective-permute-done.3
  35.3 58.9 %reduce-scatter.5.cloned.1.call-done = f32[16,2048]{1,0:T(8,128)} async-done(((f32[256,2048]{1,0:T(8,128)}), f32[16,2048]{1,0:T(8,128)}) %reduce-scatter.5.cloned.1.call-update) | async-done | bytes 131088 | tf_op jit(solution)/shard_map/reduce_scatter | solution.py:108
  94.2 1.6 multiply_reduce_fusion.1
  95.9 14.5 %all-gather = f32[32768]{0:T(1024)S(1)} all-gather(f32[2048]{0:T(1024)S(1)} %get-tuple-element.17), channel_id=2, replica_groups=mesh['section'=32,'tensor'=16] {'tensor'}, dimensions={0}, use_global_device_ids=true | all-gather | bytes 139264 | tf_op jit(solution)/shard_map/all_gather | solution.py:20
  110.6 48.2 %all-reduce = (f32[2048]{0:T(1024)S(1)}, bf16[256,16]{0,1:T(8,128)(2,1)S(1)}) all-reduce(f32[2048]{0:T(1024)S(1)} %get-tuple-element.7, f32[256,16]{0,1:T(8,128)S(1)} %fusion.7), channel_id=1, replica_groups=mesh['section'=32,'tensor'=16] {'tensor'}, use_global_device_ids=true, to_apply=%region_5.6 | all-reduce | flops 6144 | bytes 40960 | tf_op jit(solution)/shard_map/psum | solution.py:115
  159.5 4.6 %convolution_multiply_fusion = f32[256,2048]{1,0:T(8,128)} fusion(bf16[896,2048]{1,0:T(8,128)(2,1)} %copy-done.1, f32[2048]{0:T(1024)S(1)} %bitcast.38, bf16[128,896]{1,0:T(8,128)(2,1)S(1)} %get-tuple-element.19, bf16[128,896]{1,0:T(8,128)(2,1)S(1)} %get-tuple-element.20), kind=kOutput, calls=%fused_computation.3 | convolution fusion | flops 940965888 | bytes 6234112 | tf_op jit(solution)/shard_map/dot_general | solution.py:84
  164.2 3.7 %fusion.1 = f32[256,896]{1,0:T(8,128)S(1)} fusion(bf16[896,2048]{1,0:T(8,128)(2,1)} %copy-done.1, bf16[256,2048]{1,0:T(8,128)(2,1)} %all-gather.3.cloned.1.call-done, f32[2048]{0:T(1024)S(1)} %bitcast.39), kind=kOutput, calls=%fused_computation.7 | convolution fusion | flops 941096960 | bytes 5644288 | tf_op jit(solution)/shard_map/td,fd->tf/dot_general | solution.py:93
  168.0 3.4 %collective-permute-start.6 = (f32[128,896]{1,0:T(8,128)S(1)}, f32[128,896]{1,0:T(8,128)S(1)}, u32[]{:S(2)}, u32[]{:S(2)}) collective-permute-start(f32[128,896]{1,0:T(8,128)S(1)} %constant_dynamic-slice_fusion), channel_id=1, source_target_pairs={{0,16},{16,0},{32,48},{48,32},{64,80},{80,64},{96,112},{112,96},{1... | collective-permute-start | bytes 1376264 | tf_op jit(solution)/shard_map/ppermute | solution.py:10
  171.4 3.6 %collective-permute-start = (bf16[16,2048]{1,0:T(8,128)(2,1)S(1)}, bf16[16,2048]{1,0:T(8,128)(2,1)S(1)}, u32[]{:S(2)}, u32[]{:S(2)}) collective-permute-start(bf16[16,2048]{1,0:T(8,128)(2,1)S(1)} %bitcast.46), channel_id=1, source_target_pairs={{0,32},{16,48},{32,64},{48,80},{64,96},{80,112},{96,128},{112,144}... | collective-permute-start | bytes 196616 | tf_op jit(solution)/shard_map/ppermute | solution.py:16
  175.4 2.4 %collective-permute-start.5 = (f32[256,16]{0,1:T(8,128)S(1)}, f32[256,16]{0,1:T(8,128)S(1)}, u32[]{:S(2)}, u32[]{:S(2)}) collective-permute-start(f32[256,16]{0,1:T(8,128)S(1)} %fusion.2), channel_id=1, source_target_pairs={{0,16},{16,0},{32,48},{48,32},{64,80},{80,64},{96,112},{112,96},{1... | collective-permute-start | bytes 49160 | tf_op jit(solution)/shard_map/ppermute | solution.py:10
  177.9 0.9 convolution_bitcast_fusion
  178.8 2.2 collective-permute-done.5
  181.1 0.8 convolution_bitcast_fusion.1
  181.9 0.7 fusion.6
  182.6 2.2 collective-permute-done
  184.8 40.1 %reduce-scatter.3.cloned.1.call-done = f32[16,2048]{1,0:T(8,128)} async-done(((f32[256,2048]{1,0:T(8,128)}), f32[16,2048]{1,0:T(8,128)}) %reduce-scatter.3.cloned.1.call-update) | async-done | bytes 131088 | tf_op jit(solution)/shard_map/reduce_scatter | solution.py:24
  224.9 1.6 fusion.9
  (37 shorter events, 3.0 us)
Async XLA Ops:
  7.2 10.2 %copy-start = (bf16[1,16,2048]{2,1,0:T(8,128)(2,1)S(1)}, bf16[1,16,2048]{2,1,0:T(8,128)(2,1)}, u32[]{:S(2)}) copy-start(bf16[1,16,2048]{2,1,0:T(8,128)(2,1)} %param.12) | copy-start | bytes 196612
  7.2 87.1 %reduce-scatter.5.cloned.1.call-start = ((), (), s32[]{:S(2)}) async-start(), calls=%async_computation.3 | async-start | bytes 2228224 | tf_op jit(solution)/shard_map/reduce_scatter | solution.py:108
  7.2 9.4 %collective-permute-start.2 = (bf16[8,896]{1,0:T(8,128)(2,1)}, bf16[8,896]{1,0:T(8,128)(2,1)S(1)}, u32[]{:S(2)}, u32[]{:S(2)}) collective-permute-start(bf16[8,896]{1,0:T(8,128)(2,1)} %bitcast.43), channel_id=1, source_target_pairs={{0,16},{16,0},{32,48},{48,32},{64,80},{80,64},{96,112},{112,96},{1... | collective-permute-start | bytes 43016 | tf_op jit(solution)/shard_map/ppermute | solution.py:10
  10.7 10.6 %collective-permute-start.4 = (bf16[128,896]{1,0:T(8,128)(2,1)}, bf16[128,896]{1,0:T(8,128)(2,1)S(1)}, u32[]{:S(2)}, u32[]{:S(2)}) collective-permute-start(bf16[128,896]{1,0:T(8,128)(2,1)} %bitcast.36), channel_id=1, source_target_pairs={{0,16},{16,0},{32,48},{48,32},{64,80},{80,64},{96,112},{112,96},{1... | collective-permute-start | bytes 688136 | tf_op jit(solution)/shard_map/ppermute | solution.py:10
  13.1 11.7 %collective-permute-start.1 = (bf16[128,896]{1,0:T(8,128)(2,1)}, bf16[128,896]{1,0:T(8,128)(2,1)S(1)}, u32[]{:S(2)}, u32[]{:S(2)}) collective-permute-start(bf16[128,896]{1,0:T(8,128)(2,1)} %bitcast.37), channel_id=1, source_target_pairs={{0,16},{16,0},{32,48},{48,32},{64,80},{80,64},{96,112},{112,96},{1... | collective-permute-start | bytes 688136 | tf_op jit(solution)/shard_map/ppermute | solution.py:10
  17.3 7.5 %copy-start.3 = (bf16[1,128,896]{2,1,0:T(8,128)(2,1)S(1)}, bf16[1,128,896]{2,1,0:T(8,128)(2,1)}, u32[]{:S(2)}) copy-start(bf16[1,128,896]{2,1,0:T(8,128)(2,1)} %param.17) | copy-start | bytes 688132
  17.3 7.5 %copy-start.4 = (bf16[1,128,896]{2,1,0:T(8,128)(2,1)S(1)}, bf16[1,128,896]{2,1,0:T(8,128)(2,1)}, u32[]{:S(2)}) copy-start(bf16[1,128,896]{2,1,0:T(8,128)(2,1)} %param.14) | copy-start | bytes 688132
  20.7 4.2 %copy-start.1 = (bf16[896,2048]{1,0:T(8,128)(2,1)}, bf16[896,2048]{1,0:T(8,128)(2,1)S(1)}, u32[]{:S(2)}) copy-start(bf16[896,2048]{1,0:T(8,128)(2,1)S(1)} %get-tuple-element.18) | copy-start | bytes 11010052
  24.9 2.8 %copy-start.7 = (bf16[1,16,2048]{2,1,0:T(8,128)(2,1)S(1)}, bf16[1,16,2048]{2,1,0:T(8,128)(2,1)}, u32[]{:S(2)}) copy-start(bf16[1,16,2048]{2,1,0:T(8,128)(2,1)} %param.18) | copy-start | bytes 196612
  24.9 69.3 %copy-start.5 = (bf16[16,4096]{1,0:T(8,128)(2,1)S(1)}, bf16[16,4096]{1,0:T(8,128)(2,1)}, u32[]{:S(2)}) copy-start(bf16[16,4096]{1,0:T(8,128)(2,1)} %param.19) | copy-start | bytes 393220
  24.9 134.5 %copy-start.6 = (f32[1,2048]{1,0:T(1,128)S(1)}, f32[1,2048]{1,0:T(1,128)}, u32[]{:S(2)}) copy-start(f32[1,2048]{1,0:T(1,128)} %param.13) | copy-start | bytes 24580
  27.6 136.6 %all-gather.3.cloned.1.call-start = ((), (), s32[]{:S(2)}) async-start(), calls=%async_computation.4 | async-start | bytes 1114112 | tf_op jit(solution)/shard_map/all_gather | solution.py:91
  27.7 7.6 %collective-permute-start.3 = (bf16[16,2048]{1,0:T(8,128)(2,1)S(1)}, bf16[16,2048]{1,0:T(8,128)(2,1)S(1)}, u32[]{:S(2)}, u32[]{:S(2)}) collective-permute-start(bf16[16,2048]{1,0:T(8,128)(2,1)S(1)} %bitcast.45), channel_id=1, source_target_pairs={{32,0},{48,16},{64,32},{80,48},{96,64},{112,80},{128,96},{144,112}... | collective-permute-start | bytes 196616 | tf_op jit(solution)/shard_map/ppermute | solution.py:16
  95.8 129.1 %reduce-scatter.3.cloned.1.call-start = ((), (), s32[]{:S(2)}) async-start(), calls=%async_computation.2 | async-start | bytes 2228224 | tf_op jit(solution)/shard_map/reduce_scatter | solution.py:24
  164.2 7.2 %copy-start.8 = (bf16[1,16,2048]{2,1,0:T(8,128)(2,1)S(1)}, bf16[1,16,2048]{2,1,0:T(8,128)(2,1)}, u32[]{:S(2)}) copy-start(bf16[1,16,2048]{2,1,0:T(8,128)(2,1)} %param.15) | copy-start | bytes 196612
  164.2 10.9 %copy-start.2 = (bf16[256,2048]{1,0:T(8,128)(2,1)S(1)}, bf16[256,2048]{1,0:T(8,128)(2,1)}, u32[]{:S(2)}) copy-start(bf16[256,2048]{1,0:T(8,128)(2,1)} %all-gather.3.cloned.1.call-done) | copy-start | bytes 3145732
  168.0 13.9 %collective-permute-start.6 = (f32[128,896]{1,0:T(8,128)S(1)}, f32[128,896]{1,0:T(8,128)S(1)}, u32[]{:S(2)}, u32[]{:S(2)}) collective-permute-start(f32[128,896]{1,0:T(8,128)S(1)} %constant_dynamic-slice_fusion), channel_id=1, source_target_pairs={{0,16},{16,0},{32,48},{48,32},{64,80},{80,64},{96,112},{112,96},{1... | collective-permute-start | bytes 1376264 | tf_op jit(solution)/shard_map/ppermute | solution.py:10
  171.4 13.4 %collective-permute-start = (bf16[16,2048]{1,0:T(8,128)(2,1)S(1)}, bf16[16,2048]{1,0:T(8,128)(2,1)S(1)}, u32[]{:S(2)}, u32[]{:S(2)}) collective-permute-start(bf16[16,2048]{1,0:T(8,128)(2,1)S(1)} %bitcast.46), channel_id=1, source_target_pairs={{0,32},{16,48},{32,64},{48,80},{64,96},{80,112},{96,128},{112,144}... | collective-permute-start | bytes 196616 | tf_op jit(solution)/shard_map/ppermute | solution.py:16
  175.4 5.6 %collective-permute-start.5 = (f32[256,16]{0,1:T(8,128)S(1)}, f32[256,16]{0,1:T(8,128)S(1)}, u32[]{:S(2)}, u32[]{:S(2)}) collective-permute-start(f32[256,16]{0,1:T(8,128)S(1)} %fusion.2), channel_id=1, source_target_pairs={{0,16},{16,0},{32,48},{48,32},{64,80},{80,64},{96,112},{112,96},{1... | collective-permute-start | bytes 49160 | tf_op jit(solution)/shard_map/ppermute | solution.py:10
Sparse Core Ops, SparseCore 0:
  27.7 66.4 reduce-scatter.4
  96.9 39.5 all-gather.2
  164.3 60.6 reduce-scatter.2
